TPU v7x, 256 devices: a whole 4x4x8 slice. The times are simulated.
256 devices in a mesh: dp: 128 (over x, y, z_hi, core), tp: 2 (over z_lo).
Axes of the slice: x: 4, y: 4, z: 8 (z_hi: 4, z_lo: 2; z = z_hi * 2 + z_lo), core: 2. Of those that a mesh axis runs over, the one named last changes fastest.
Arguments:
- tokens: bfloat16 [256, 512, 768], P('dp', 'tp'), may hold values from -6 to 6
- eval_tokens: bfloat16 [256, 512, 768], P('dp', 'tp'), may hold values from -6 to 6
- cotangent: bfloat16 [256, 512, 768], P('dp', 'tp'), may hold values from -6 to 6
- lengths: int32 [256], P('dp'), may hold values from 1 to 512, as said below
- w_query: bfloat16 [768, 768], P(('dp', 'tp')), may hold values from -0.21875 to 0.21875
- w_key: bfloat16 [768, 768], P(('dp', 'tp')), may hold values from -0.21875 to 0.21875
- w_value: bfloat16 [768, 768], P(('dp', 'tp')), may hold values from -0.21875 to 0.21875
- w_out: bfloat16 [768, 768], P(('dp', 'tp')), may hold values from -3.5 to 3.5
- w_up: bfloat16 [768, 3072], P('dp', 'tp'), may hold values from -0.21875 to 0.21875
- w_down: bfloat16 [3072, 768], P('tp', 'dp'), may hold values from -0.109375 to 0.109375
- a_query: bfloat16 [768, 8], P(('dp', 'tp')), may hold values from -0.21875 to 0.21875
- a_value: bfloat16 [768, 8], P(('dp', 'tp')), may hold values from -0.21875 to 0.21875
- query_up_weight: bfloat16 [8, 768], replicated, may hold values from -0.59765625 to 0.59765625
- value_up_weight: bfloat16 [8, 768], replicated, may hold values from -0.59765625 to 0.59765625
- query_bias_vector: bfloat16 [768], replicated, may hold values from -1.796875 to 1.796875
- value_bias_vector: bfloat16 [768], replicated, may hold values from -0.29882812 to 0.29882812
- bias_out: bfloat16 [768], replicated, may hold values from -1.796875 to 1.796875
- bias_up: bfloat16 [3072], replicated, may hold values from -1.796875 to 1.796875
- bias_down: bfloat16 [768], replicated, may hold values from -1.796875 to 1.796875
- gain_one: bfloat16 [768], replicated, may hold values from 0.5 to 1.5
- shift_one: bfloat16 [768], replicated, may hold values from -1.796875 to 1.796875
- gain_two: bfloat16 [768], replicated, may hold values from 0.5 to 1.5
- shift_two: bfloat16 [768], replicated, may hold values from -1.796875 to 1.796875
Outputs:
- activations: bfloat16 [256, 512, 768], P('dp', 'tp')
- input_grad: float32 [256, 512, 768], P('dp', 'tp')
- grad_b_query: float32 [8, 768], replicated
- grad_b_value: float32 [8, 768], replicated
- eval_output: bfloat16 [256, 512, 768], P('dp', 'tp')
Inputs may be any that keep to these rules, and one draw needn't show every extreme that they name: `lengths`: of the 2 items of each index of dp (items k * 2 to k * 2 + 1), at least one has length 512; the others are drawn evenly.
All inputs are finite; a program needn't handle non-finite values.
Results may differ from a plain program's by a relative error of at most 0.015.
Values may be sent and summed in bfloat16 or wider, within the bound.
A program may use at most 128 MiB of HBM per device.

v0:
```python
import math

import jax
import jax.numpy as jnp
from jax import lax
from jax.sharding import PartitionSpec as P

HEADS = 12


EPSILON = 1e-05


def in_one_piece(arrays, axis, dim, along):
    widths = [a.shape[along] for a in arrays]
    both = jnp.concatenate(arrays, axis=along)
    whole = lax.all_gather(both, axis, axis=dim, tiled=True)
    return tuple(jnp.split(whole, [sum(widths[:k]) for k in range(1, len(widths))], axis=along))


def rows_first(arrays, axis, dims):
    turned = [jnp.moveaxis(a, dim, 0) for a, dim in zip(arrays, dims)]
    both = jnp.concatenate([t.reshape(len(t), -1) for t in turned], axis=1)
    whole, at, outs = (lax.all_gather(both, axis, axis=0, tiled=True), 0, [])
    for t, dim in zip(turned, dims):
        section = whole[:, at : at + t[0].size].reshape(-1, *t.shape[1:])
        outs.append(jnp.moveaxis(section, 0, dim))
        at += t[0].size
    return tuple(outs)


def laid_out(parts, dim):
    parts = jnp.moveaxis(parts, 0, dim)
    lengths = parts.shape
    return parts.reshape(*lengths[:dim], lengths[dim] * lengths[dim + 1], *lengths[dim + 2 :])


def copy_for_each(x, axis):
    copies = jnp.broadcast_to(x, (lax.axis_size(axis), *x.shape))
    return lax.all_to_all(copies, axis, split_axis=0, concat_axis=0, tiled=True)


def gather_directly(x, axis, dim):
    return laid_out(copy_for_each(x, axis), dim)


def cut_along(x, dim, count):
    before, after = (x.shape[:dim], x.shape[dim + 1 :])
    return jnp.moveaxis(x.reshape(*before, count, -1, *after), dim, 0)


def summed_on_arrival(x, axis, dim):
    parts = cut_along(x, dim, lax.axis_size(axis))
    arrived = lax.all_to_all(parts, axis, split_axis=0, concat_axis=0, tiled=True)
    return arrived.astype(jnp.float32).sum(axis=0)


def in_one_piece_2(arrays, axis, dim, along):
    both = jnp.concatenate(arrays, axis=along)
    whole, at, outs = (summed_on_arrival(both, axis, dim), 0, [])
    for a in arrays:
        outs.append(lax.slice_in_dim(whole, at, at + a.shape[along], axis=along))
        at += a.shape[along]
    return tuple(outs)


def norm_rows(matrix_rows, gain_vec, shift_vec):
    row_mean = jnp.mean(matrix_rows, axis=-1, keepdims=True)
    centred = matrix_rows - row_mean
    spread = jnp.mean(centred * centred, axis=-1, keepdims=True)
    return centred * lax.rsqrt(spread + EPSILON) * gain_vec + shift_vec


def gelu_exact(pre_values):
    return jax.nn.gelu(pre_values, approximate=False)


def split_heads(tensor_in):
    lead_count, seq_len, model_width = tensor_in.shape
    return tensor_in.reshape(lead_count, seq_len, HEADS, model_width // HEADS)


def score_block(query_heads, key_heads, key_mask_valid):
    score_scale = 1.0 / math.sqrt(query_heads.shape[-1])
    raw_scores = (
        jnp.einsum("nqhe,nkhe->nhqk", query_heads, key_heads, preferred_element_type=jnp.float32)
        * score_scale
    )
    return jnp.where(key_mask_valid[:, None, None, :], raw_scores, -1e30)


def shards(
    tokens,
    eval_tokens,
    cotangent,
    lengths,
    w_query,
    w_key,
    w_value,
    w_out,
    w_up,
    w_down,
    a_query,
    a_value,
    query_up_weight,
    value_up_weight,
    query_bias_vector,
    value_bias_vector,
    bias_out,
    bias_up,
    bias_down,
    gain_one,
    shift_one,
    gain_two,
    shift_two,
):
    item_count, half_rows, model_width = tokens.shape
    seq_len = half_rows * lax.axis_size("tp")
    offset = lax.axis_index("tp") * half_rows
    key_mask_valid = jnp.arange(seq_len, dtype=jnp.int32)[None, :] < lengths[:, None]
    query_valid = (offset + jnp.arange(half_rows, dtype=jnp.int32))[None, :] < lengths[:, None]
    pair_parts = in_one_piece((w_query, w_key, w_value, w_out, a_query, a_value), "tp", 0, 1)
    (
        query_weight_matrix,
        key_mat,
        value_weight_matrix,
        out_mat,
        query_down_weight,
        value_down_weight,
    ) = in_one_piece(
        (pair_parts[0], pair_parts[1], pair_parts[2], pair_parts[3], pair_parts[4], pair_parts[5]),
        "dp",
        0,
        1,
    )
    up_cols, down_rows = rows_first((w_up, w_down), "dp", (0, 1))
    up_mat, down_mat = (up_cols, down_rows)
    hidden_part = up_cols.shape[1]
    up_bias = lax.dynamic_slice_in_dim(
        bias_up, lax.axis_index("tp") * hidden_part, hidden_part
    ).astype(jnp.float32)
    score_scale = 1.0 / math.sqrt(model_width // HEADS)

    def feed_forward(normed):
        normed_low = normed.astype(jnp.bfloat16)
        gathered = gather_directly(normed_low, "tp", 1)
        hidden_pre = jnp.dot(gathered, up_mat, preferred_element_type=jnp.float32) + up_bias
        hidden_act = gelu_exact(hidden_pre).astype(jnp.bfloat16)
        partial_value = jnp.dot(hidden_act, down_mat, preferred_element_type=jnp.float32)
        branch_out = summed_on_arrival(partial_value.astype(jnp.bfloat16), "tp", 1)
        return (branch_out + bias_down.astype(jnp.float32), hidden_pre)

    def forward_pass(input_rows, query_effective, value_effective, enable_adapter):
        query_preactivation = jnp.dot(
            input_rows, query_effective, preferred_element_type=jnp.float32
        ) + query_bias_vector.astype(jnp.float32)
        value_preactivation = jnp.dot(
            input_rows, value_effective, preferred_element_type=jnp.float32
        ) + value_bias_vector.astype(jnp.float32)
        low_query = None
        low_value = None
        if enable_adapter:
            low_query = jnp.dot(
                input_rows, query_down_weight, preferred_element_type=jnp.float32
            ).astype(jnp.bfloat16)
            low_value = jnp.dot(
                input_rows, value_down_weight, preferred_element_type=jnp.float32
            ).astype(jnp.bfloat16)
            query_preactivation = query_preactivation + 2.0 * jnp.dot(
                low_query, query_up_weight, preferred_element_type=jnp.float32
            )
            value_preactivation = value_preactivation + 2.0 * jnp.dot(
                low_value, value_up_weight, preferred_element_type=jnp.float32
            )
        query_low = query_preactivation.astype(jnp.bfloat16)
        key_low = jnp.dot(input_rows, key_mat, preferred_element_type=jnp.float32).astype(
            jnp.bfloat16
        )
        value_low = value_preactivation.astype(jnp.bfloat16)
        keys_all, values_all = in_one_piece((key_low, value_low), "tp", 1, 0)
        query_heads = split_heads(query_low)
        key_heads = split_heads(keys_all)
        value_heads = split_heads(values_all)
        masked = score_block(query_heads, key_heads, key_mask_valid)
        row_max = jnp.max(masked, axis=-1, keepdims=True)
        exp_scores = jnp.exp(masked - row_max)
        exp_total = jnp.sum(exp_scores, axis=-1, keepdims=True)
        prob_low = (exp_scores / exp_total).astype(jnp.bfloat16)
        attn_mix = jnp.einsum(
            "nhqk,nkhe->nqhe", prob_low, value_heads, preferred_element_type=jnp.float32
        )
        attn_mix = attn_mix.reshape(item_count, half_rows, model_width).astype(jnp.bfloat16)
        first_sum = (
            input_rows.astype(jnp.float32)
            + jnp.dot(attn_mix, out_mat, preferred_element_type=jnp.float32)
            + bias_out.astype(jnp.float32)
        )
        normed = norm_rows(first_sum, gain_one.astype(jnp.float32), shift_one.astype(jnp.float32))
        branch_out, hidden_pre = feed_forward(normed)
        second_sum = normed + branch_out
        layer_result = norm_rows(
            second_sum, gain_two.astype(jnp.float32), shift_two.astype(jnp.float32)
        )
        kept_state = (
            low_query,
            low_value,
            query_heads,
            key_heads,
            value_heads,
            row_max + jnp.log(exp_total),
            first_sum,
            second_sum,
            hidden_pre,
        )
        return (layer_result, kept_state)

    layer_result, kept_state = forward_pass(tokens, query_weight_matrix, value_weight_matrix, True)
    (
        low_query,
        low_value,
        query_heads,
        key_heads,
        value_heads,
        log_total,
        first_sum,
        second_sum,
        hidden_pre,
    ) = kept_state
    grad_out = cotangent.astype(jnp.float32) * query_valid[:, :, None].astype(jnp.float32)
    norm_two = jax.vjp(
        lambda rows_in: norm_rows(
            rows_in, gain_two.astype(jnp.float32), shift_two.astype(jnp.float32)
        ),
        second_sum,
    )[1]
    grad_second = norm_two(grad_out)[0]
    grad_branch = grad_second.astype(jnp.bfloat16)
    grad_rows = gather_directly(grad_branch, "tp", 1)
    grad_act = jnp.einsum("nsd,fd->nsf", grad_rows, down_mat, preferred_element_type=jnp.float32)
    grad_pre = jax.vjp(gelu_exact, hidden_pre)[1](grad_act)[0]
    grad_terms = jnp.einsum(
        "nsf,df->nsd", grad_pre.astype(jnp.bfloat16), up_mat, preferred_element_type=jnp.float32
    )
    grad_hidden = summed_on_arrival(grad_terms.astype(jnp.bfloat16), "tp", 1)
    grad_normed = grad_second + grad_hidden
    norm_one = jax.vjp(
        lambda rows_in: norm_rows(
            rows_in, gain_one.astype(jnp.float32), shift_one.astype(jnp.float32)
        ),
        first_sum,
    )[1]
    grad_first = norm_one(grad_normed)[0]
    grad_attn_low = grad_first.astype(jnp.bfloat16)
    grad_mix = jnp.einsum(
        "nsd,ed->nse", grad_attn_low, out_mat, preferred_element_type=jnp.float32
    ).astype(jnp.bfloat16)
    grad_heads = split_heads(grad_mix)
    masked = score_block(query_heads, key_heads, key_mask_valid)
    attn_prob = jnp.exp(masked - log_total)
    grad_prob = jnp.einsum(
        "nqhe,nkhe->nhqk", grad_heads, value_heads, preferred_element_type=jnp.float32
    )
    inner_sum = jnp.sum(attn_prob * grad_prob, axis=-1, keepdims=True)
    grad_score_low = (attn_prob * (grad_prob - inner_sum)).astype(jnp.bfloat16)
    grad_query = (
        jnp.einsum("nhqk,nkhe->nqhe", grad_score_low, key_heads, preferred_element_type=jnp.float32)
        * score_scale
    )
    grad_query = grad_query.reshape(item_count, half_rows, model_width).astype(jnp.bfloat16)
    key_terms = (
        jnp.einsum(
            "nhqk,nqhe->nkhe", grad_score_low, query_heads, preferred_element_type=jnp.float32
        )
        * score_scale
    )
    value_terms = jnp.einsum(
        "nhqk,nqhe->nkhe",
        attn_prob.astype(jnp.bfloat16),
        grad_heads,
        preferred_element_type=jnp.float32,
    )
    grad_key, grad_value = in_one_piece_2(
        (
            key_terms.reshape(item_count, seq_len, model_width).astype(jnp.bfloat16),
            value_terms.reshape(item_count, seq_len, model_width).astype(jnp.bfloat16),
        ),
        "tp",
        1,
        0,
    )
    grad_key = grad_key.astype(jnp.bfloat16)
    grad_value = grad_value.astype(jnp.bfloat16)
    grad_low_query = 2.0 * jnp.einsum(
        "nsd,rd->nsr", grad_query, query_up_weight, preferred_element_type=jnp.float32
    )
    grad_low_value = 2.0 * jnp.einsum(
        "nsd,rd->nsr", grad_value, value_up_weight, preferred_element_type=jnp.float32
    )
    input_grad = grad_first
    input_grad = input_grad + jnp.einsum(
        "nsd,ed->nse", grad_query, query_weight_matrix, preferred_element_type=jnp.float32
    )
    input_grad = input_grad + jnp.einsum(
        "nsd,ed->nse", grad_key, key_mat, preferred_element_type=jnp.float32
    )
    input_grad = input_grad + jnp.einsum(
        "nsd,ed->nse", grad_value, value_weight_matrix, preferred_element_type=jnp.float32
    )
    input_grad = input_grad + jnp.einsum(
        "nsr,dr->nsd",
        grad_low_query,
        query_down_weight.astype(jnp.float32),
        precision=lax.Precision.HIGHEST,
    )
    input_grad = input_grad + jnp.einsum(
        "nsr,dr->nsd",
        grad_low_value,
        value_down_weight.astype(jnp.float32),
        precision=lax.Precision.HIGHEST,
    )
    local_query = 2.0 * jnp.einsum(
        "nsr,nsd->rd", low_query, grad_query, preferred_element_type=jnp.float32
    )
    local_value = 2.0 * jnp.einsum(
        "nsr,nsd->rd", low_value, grad_value, preferred_element_type=jnp.float32
    )
    grad_b_query, grad_b_value = lax.psum((local_query, local_value), ("dp", "tp"))
    merged_query = (
        query_weight_matrix.astype(jnp.float32)
        + 2.0 * jnp.dot(query_down_weight, query_up_weight, preferred_element_type=jnp.float32)
    ).astype(jnp.bfloat16)
    merged_value = (
        value_weight_matrix.astype(jnp.float32)
        + 2.0 * jnp.dot(value_down_weight, value_up_weight, preferred_element_type=jnp.float32)
    ).astype(jnp.bfloat16)
    eval_result, unused_state = forward_pass(eval_tokens, merged_query, merged_value, False)
    return (
        layer_result.astype(jnp.bfloat16),
        input_grad,
        grad_b_query,
        grad_b_value,
        eval_result.astype(jnp.bfloat16),
    )


def solution(mesh):
    in_specs = (
        P("dp", "tp", None),
        P("dp", "tp", None),
        P("dp", "tp", None),
        P("dp"),
        P(("dp", "tp"), None),
        P(("dp", "tp"), None),
        P(("dp", "tp"), None),
        P(("dp", "tp"), None),
        P("dp", "tp"),
        P("tp", "dp"),
        P(("dp", "tp"), None),
        P(("dp", "tp"), None),
        P(),
        P(),
        P(),
        P(),
        P(),
        P(),
        P(),
        P(),
        P(),
        P(),
        P(),
    )
    out_specs = (P("dp", "tp", None), P("dp", "tp", None), P(), P(), P("dp", "tp", None))
    return jax.shard_map(shards, mesh=mesh, in_specs=in_specs, out_specs=out_specs, check_vma=False)
```

profile of v0, /device:TPU:1, one launch (start us, length us, event | category | flops | bytes accessed | tf_op | source)
XLA Modules:
  0.0 668.4 jit_solution(17209261675794579492)
XLA Ops:
  8.1 4.3 all-gather
  13.8 88.5 %all-gather.12.cloned.1.call-done = bf16[128,6,3088]{2,1,0:T(8,128)(2,1)} async-done(((bf16[1,6,3088]{2,1,0:T(8,128)(2,1)}), bf16[128,6,3088]{2,1,0:T(8,128)(2,1)}) %all-gather.12.cloned.1.call-update) | async-done | bytes 4743184 | tf_op jit(solution)/shard_map/all_gather | solution.py:17
  102.4 9.9 %reshape.223 = bf16[768,3088]{1,0:T(8,128)(2,1)} reshape(bf16[128,6,3088]{2,1,0:T(8,128)(2,1)} %all-gather.12.cloned.1.call-done) | data formatting | bytes 9486336
  114.1 3.0 fusion.58
  117.8 3.3 fusion.56
  121.1 2.7 pad_maximum_fusion.1
  140.3 3.6 add_convert_fusion.4
  144.4 27.7 %all-gather.10.cloned.1.call-done = bf16[4,512,768]{1,2,0:T(8,128)(2,1)} async-done(((bf16[4,256,768]{1,2,0:T(8,128)(2,1)}), bf16[4,512,768]{1,2,0:T(8,128)(2,1)}) %all-gather.10.cloned.1.call-update) | async-done | bytes 3145744 | tf_op jit(solution)/shard_map/all_gather | solution.py:17
  172.1 3.3 fusion.153
  175.4 10.0 %fusion.156 = (f32[2,12,256]{2,1,0:T(8,128)S(1)}, f32[2,12,256,512]{3,2,1,0:T(8,128)}) fusion(pred[2,512]{1,0:T(4,128)(4,1)S(1)} %copy-done.20, bf16[2,256,12,64]{1,3,2,0:T(8,128)(2,1)S(1)} %bitcast.230, bf16[2,512,12,64]{1,3,2,0:T(8,128)(2,1)} %bitcast.227), kind=kOutput, calls=%fused_computation.250 | convolution fusion | flops 415236608 | bytes 14967808 | tf_op jit(solution)/shard_map/sub | solution.py:186
  185.4 7.0 %fusion.54 = bf16[2,12,64,256]{3,2,1,0:T(8,128)(2,1)S(1)} fusion(bf16[2,512,12,64]{1,3,2,0:T(8,128)(2,1)S(1)} %bitcast.226, f32[2,12,256,512]{3,2,1,0:T(8,128)} %get-tuple-element.40, f32[2,12,256]{2,1,0:T(8,128)S(1)} %get-tuple-element.39), kind=kOutput, calls=%fused_computation.125 | convolution fusion | flops 409337856 | bytes 14966784 | tf_op jit(solution)/shard_map/nhqk,nkhe->nqhe/dot_general | solution.py:189
  194.9 30.0 %all-gather.8.cloned.1.call-done = bf16[4,512,768]{1,2,0:T(8,128)(2,1)} async-done(((bf16[4,256,768]{1,2,0:T(8,128)(2,1)}), bf16[4,512,768]{1,2,0:T(8,128)(2,1)}) %all-gather.8.cloned.1.call-update) | async-done | bytes 3145744 | tf_op jit(solution)/shard_map/all_gather | solution.py:17
  229.3 3.1 fusion.1
  233.9 5.0 fusion.55
  242.1 22.6 %all_to_all.35 = bf16[2,2,256,768]{3,2,1,0:T(8,128)(2,1)} all-to-all(bf16[2,2,256,768]{3,2,1,0:T(8,128)(2,1)S(1)} %broadcast_in_dim.42), channel_id=1, replica_groups=mesh['dp'=128,'tp'=2] {'tp'}, dimensions={0} | all-to-all | bytes 3145728 | tf_op jit(solution)/shard_map/all_to_all | solution.py:40
  266.0 3.7 all-to-all-start
  269.7 44.9 %all-gather.14.cloned.1.call-done = bf16[128,6,3072]{2,1,0:T(8,128)(2,1)} async-done(((bf16[1,6,3072]{2,1,0:T(8,128)(2,1)}), bf16[128,6,3072]{2,1,0:T(8,128)(2,1)}) %all-gather.14.cloned.1.call-update) | async-done | bytes 4718608 | tf_op jit(solution)/shard_map/all_gather | solution.py:24
  314.7 7.8 %reshape.225 = bf16[768,3072]{1,0:T(8,128)(2,1)} reshape(bf16[128,6,3072]{2,1,0:T(8,128)(2,1)} %all-gather.14.cloned.1.call-done) | data formatting | bytes 9437184
  322.5 2.6 copy.85
  325.2 4.4 fusion.63
  329.7 11.4 %fusion.47 = (u8[512,1536]{1,0:T(8,128)(4,1)S(1)}, u8[512,1536]{1,0:T(8,128)(4,1)S(1)}, u8[512,1536]{1,0:T(8,128)(4,1)}, u8[512,1536]{1,0:T(8,128)(4,1)}, f32[2,512,1536]{2,1,0:T(8,128)}) fusion(f32[1536]{0:T(1024)S(1)} %dynamic-slice_convert_fusion, f32[2,512,1536]{2,1,0:T(8,128)S(1)} %fusion.63, bf16[2,512,768]{2,1,0:T(8,128)(2,1)S(1)} %bitcast.220, ...), kind=kOutput, calls=%fused_computation.115 | convolution fusion | flops 2456813568 | bytes 19668992 | tf_op jit(solution)/shard_map/dot_general | solution.py:147
  341.1 19.2 %fusion.34 = bf16[2,512,768]{2,1,0:T(8,128)(2,1)S(1)} fusion(f32[2,512,1536]{2,1,0:T(8,128)} %get-tuple-element.43, f32[1536]{0:T(1024)S(1)} %dynamic-slice_convert_fusion, bf16[768,3072]{1,0:T(8,128)(2,1)S(1)} %bitcast.217, u8[512,1536]{1,0:T(8,128)(4,1)S(1)} %get-tuple-element.6, u8[512,1536]{1,0:T(8,128)(4,1)S(1)} %get-tuple-element.5), kind=kOutput, calls=%fused_computation.79 | convolution fusion | flops 2528378880 | bytes 11804672 | tf_op jit(solution)/shard_map/dot_general | solution.py:149
  361.5 3.7 all-to-all-start.6
  365.2 15.5 %fusion.4 = f32[2,512,1536]{2,1,0:T(8,128)S(1)} fusion(f32[2,512,1536]{2,1,0:T(8,128)} %copy-done.11, f32[1536]{0:T(1024)S(1)} %dynamic-slice_convert_fusion, u8[512,1536]{1,0:T(8,128)(4,1)} %get-tuple-element.11, u8[512,1536]{1,0:T(8,128)(4,1)} %get-tuple-element.12), kind=kLoop, calls=%fused_computation.15 | loop fusion | flops 106954752 | bytes 14161920 | tf_op jit(solution)/shard_map/erfc | solution.py:75
  380.7 8.4 %fusion.38 = bf16[2,512,768]{2,1,0:T(8,128)(2,1)S(1)} fusion(f32[2,512,1536]{2,1,0:T(8,128)S(1)} %fusion.4, f32[2,512,1536]{2,1,0:T(8,128)} %copy-done.11, f32[1536]{0:T(1024)S(1)} %dynamic-slice_convert_fusion, bf16[768,3072]{1,0:T(8,128)(2,1)} %reshape.225), kind=kOutput, calls=%fused_computation.81 | convolution fusion | flops 2422996992 | bytes 16521216 | tf_op jit(solution)/shard_map/dot_general | solution.py:149
  390.5 4.6 all-to-all-start.1
  396.6 17.7 %all-to-all-done.1 = bf16[2,2,256,768]{3,2,1,0:T(8,128)(2,1)} async-done(((bf16[2,2,256,768]{3,2,1,0:T(8,128)(2,1)}), bf16[2,2,256,768]{3,2,1,0:T(8,128)(2,1)}, u32[]{:S(2)}, u32[]{:S(2)}) %all-to-all-start.1) | async-done | bytes 1572896 | tf_op jit(solution)/shard_map/all_to_all | solution.py:54
  416.3 3.6 fusion.149
  422.0 20.9 %all_to_all.36 = bf16[2,2,256,768]{3,2,1,0:T(8,128)(2,1)S(1)} all-to-all(bf16[2,2,256,768]{3,2,1,0:T(8,128)(2,1)S(1)} %broadcast_in_dim.39), channel_id=1, replica_groups=mesh['dp'=128,'tp'=2] {'tp'}, dimensions={0} | all-to-all | bytes 3145728 | tf_op jit(solution)/shard_map/all_to_all | solution.py:40
  444.1 13.0 %fusion.37 = bf16[2,512,768]{2,1,0:T(8,128)(2,1)} fusion(f32[2,512,1536]{2,1,0:T(8,128)} %copy-done.12, bf16[2,512,768]{2,1,0:T(8,128)(2,1)} %bitcast.221, f32[2,512,1536]{2,1,0:T(8,128)} %copy-done.11, f32[1536]{0:T(1024)S(1)} %dynamic-slice_convert_fusion, bf16[768,3072]{1,0:T(8,128)(2,1)} %reshape.225), kind=kOutput, calls=%fused_computation.80 | convolution fusion | flops 4856217600 | bytes 20453376 | tf_op jit(solution)/shard_map/nsf,df->nsd/dot_general | solution.py:241
  457.1 2.7 copy.114
  459.8 4.6 all-to-all-start.3
  466.2 15.6 %all-to-all-done.3 = bf16[2,2,256,768]{3,2,1,0:T(8,128)(2,1)} async-done(((bf16[2,2,256,768]{3,2,1,0:T(8,128)(2,1)}), bf16[2,2,256,768]{3,2,1,0:T(8,128)(2,1)}, u32[]{:S(2)}, u32[]{:S(2)}) %all-to-all-start.3) | async-done | bytes 1572896 | tf_op jit(solution)/shard_map/all_to_all | solution.py:54
  485.2 2.9 fusion.150
  491.7 6.6 fusion.48
  498.2 12.2 %multiply_reduce_fusion = (f32[2,12,256]{2,1,0:T(8,128)S(1)}, f32[2,12,256,512]{3,2,1,0:T(8,128)}) fusion(f32[2,12,256]{2,1,0:T(8,128)S(1)} %log_add_fusion, f32[2,12,256,512]{3,2,1,0:T(8,128)} %copy-done.1, pred[2,512]{1,0:T(4,128)(4,1)S(1)} %copy-done.20, bf16[2,256,12,64]{1,3,2,0:T(8,128)(2,1)S(1)} %bitcast.219, bf16[2,512,12,64]{1,3,2,0:T(8,128)(2,1)S(1)} %bitcast.209), kind=kOutput, calls=%fused_computation.5 | convolution fusion | flops 418375680 | bytes 27575296 | tf_op jit(solution)/shard_map/nqhe,nkhe->nhqk/dot_general | solution.py:260
  511.1 9.7 %multiply_convert_fusion = bf16[2,12,256,512]{3,2,1,0:T(8,128)(2,1)S(1)} fusion(f32[2,12,256,512]{3,2,1,0:T(8,128)} %get-tuple-element.45, f32[2,12,256]{2,1,0:T(8,128)S(1)} %get-tuple-element.44, f32[2,12,256]{2,1,0:T(8,128)S(1)} %log_add_fusion, f32[2,12,256,512]{3,2,1,0:T(8,128)} %copy-done.1, pred[2,512]{1,0:T(4,128)(4,1)S(1)} %copy-done.20), kind=kLoop, calls=%fused_computation.4 | loop fusion | flops 18874368 | bytes 31507456 | tf_op jit(solution)/shard_map/convert_element_type | solution.py:264
  520.8 2.7 copy-done.2
  525.8 2.4 convert_element_type.263
  530.3 5.6 all-to-all-start.4
  536.0 4.8 multiply_convert_fusion.6
  543.1 3.3 fusion.65
  546.4 22.9 %all-to-all-done.4 = bf16[2,4,256,768]{2,3,1,0:T(8,128)(2,1)} async-done(((bf16[2,4,256,768]{2,3,1,0:T(8,128)(2,1)}), bf16[2,4,256,768]{2,3,1,0:T(8,128)(2,1)}, u32[]{:S(2)}, u32[]{:S(2)}) %all-to-all-start.4) | async-done | bytes 3145760 | tf_op jit(solution)/shard_map/all_to_all | solution.py:54
  569.2 2.7 reduce
  572.4 3.3 fusion.69
  575.7 3.3 fusion.81
  579.0 76.8 %all-reduce = (f32[8,768]{1,0:T(8,128)}, f32[8,768]{1,0:T(8,128)}) all-reduce(f32[8,768]{1,0:T(8,128)S(1)} %fusion.74, f32[8,768]{1,0:T(8,128)S(1)} %fusion.73), channel_id=1, replica_groups=mesh['dp'=128,'tp'=2] {'dp','tp'}, use_global_device_ids=true, to_apply=%region_14.15 | all-reduce | flops 12288 | bytes 98304 | tf_op jit(solution)/shard_map/psum | solution.py:327
  655.8 5.5 add_add_fusion.4
  (175 shorter events, 60.5 us)
Async XLA Ops:
  7.2 133.1 %copy-start = (bf16[8,768]{1,0:T(8,128)(2,1)S(1)}, bf16[8,768]{1,0:T(8,128)(2,1)}, u32[]{:S(2)}) copy-start(bf16[8,768]{1,0:T(8,128)(2,1)} %param.35) | copy-start | bytes 36868
  7.2 95.2 %all-gather.12.cloned.1.call-start = ((), (), s32[]{:S(2)}) async-start(), calls=%async_computation.9 | async-start | bytes 6604800 | tf_op jit(solution)/shard_map/all_gather | solution.py:17
  13.1 159.0 %all-gather.10.cloned.1.call-start = ((), (), s32[]{:S(2)}) async-start(), calls=%async_computation.8 | async-start | bytes 4718592 | tf_op jit(solution)/shard_map/all_gather | solution.py:17
  121.1 2.8 copy-start.17
  123.8 3.7 copy-start.25
  123.8 101.1 %all-gather.8.cloned.1.call-start = ((), (), s32[]{:S(2)}) async-start(), calls=%async_computation.7 | async-start | bytes 4718592 | tf_op jit(solution)/shard_map/all_gather | solution.py:17
  125.4 2.1 copy-start.21
  130.1 2.7 copy-start.33
  130.1 2.7 copy-start.34
  130.1 3.3 copy-start.35
  130.1 3.9 copy-start.36
  131.4 183.3 %all-gather.14.cloned.1.call-start = ((), (), s32[]{:S(2)}) async-start(), calls=%async_computation.10 | async-start | bytes 6340608 | tf_op jit(solution)/shard_map/all_gather | solution.py:24
  140.3 3.6 copy-start.23
  140.3 3.6 copy-start.30
  144.4 82.7 %copy-start.9 = (bf16[2,256,768]{1,2,0:T(8,128)(2,1)}, bf16[2,256,768]{1,2,0:T(8,128)(2,1)S(1)}, u32[]{:S(2)}) copy-start(bf16[2,256,768]{1,2,0:T(8,128)(2,1)S(1)} %fusion.42) | copy-start | bytes 2359300
  144.4 31.0 %copy-start.20 = (pred[2,512]{1,0:T(4,128)(4,1)S(1)}, pred[2,512]{1,0:T(4,128)(4,1)}, u32[]{:S(2)}) copy-start(pred[2,512]{1,0:T(4,128)(4,1)} %iota_compare_fusion) | copy-start | bytes 3076
  144.4 31.0 %copy-start.44 = (bf16[768,2,256]{2,0,1:T(8,128)(2,1)S(1)}, bf16[768,2,256]{2,0,1:T(8,128)(2,1)}, u32[]{:S(2)}) copy-start(bf16[768,2,256]{2,0,1:T(8,128)(2,1)} %add_convert_fusion.4) | copy-start | bytes 2359300
  185.4 7.0 %copy-start.31 = (f32[768]{0:T(1024)S(1)}, f32[768]{0:T(1024)}, u32[]{:S(2)}) copy-start(f32[768]{0:T(1024)} %convert_element_type.237) | copy-start | bytes 9220
  185.4 7.0 %copy-start.43 = (bf16[2,256,768]{2,1,0:T(8,128)(2,1)S(1)}, bf16[2,256,768]{2,1,0:T(8,128)(2,1)}, u32[]{:S(2)}) copy-start(bf16[2,256,768]{2,1,0:T(8,128)(2,1)} %param.24) | copy-start | bytes 2359300
  194.6 46.8 %copy-start.5 = (f32[2,256,768]{2,1,0:T(8,128)}, f32[2,256,768]{2,1,0:T(8,128)S(1)}, u32[]{:S(2)}) copy-start(f32[2,256,768]{2,1,0:T(8,128)S(1)} %get-tuple-element.42) | copy-start | bytes 4718596
  227.0 2.3 copy-start.6
  227.0 5.4 copy-start.13
  229.3 4.5 copy-start.1
  233.8 5.0 copy-start.18
  238.8 2.6 copy-start.27
  264.7 4.9 copy-start.32
  266.0 59.1 %all-to-all-start = ((bf16[2,2,256,768]{3,2,1,0:T(8,128)(2,1)}), bf16[2,2,256,768]{3,2,1,0:T(8,128)(2,1)S(1)}, u32[]{:S(2)}, u32[]{:S(2)}) async-start(bf16[2,2,256,768]{3,2,1,0:T(8,128)(2,1)} %broadcast_in_dim.36), calls=%async_computation | async-start | bytes 3145728 | tf_op jit(solution)/shard_map/all_to_all | solution.py:40
  325.1 4.6 slice-start
  325.2 4.5 slice-start.1
  325.2 4.5 copy-start.19
  329.6 11.5 %copy-start.11 = (f32[2,512,1536]{2,1,0:T(8,128)}, f32[2,512,1536]{2,1,0:T(8,128)S(1)}, u32[]{:S(2)}) copy-start(f32[2,512,1536]{2,1,0:T(8,128)S(1)} %fusion.63) | copy-start | bytes 18874372
  361.5 29.0 %all-to-all-start.6 = ((bf16[2,2,256,768]{3,2,1,0:T(8,128)(2,1)}), bf16[2,2,256,768]{3,2,1,0:T(8,128)(2,1)S(1)}, u32[]{:S(2)}, u32[]{:S(2)}) async-start(bf16[2,2,256,768]{3,2,1,0:T(8,128)(2,1)} %bitcast.214), calls=%async_computation.6 | async-start | bytes 3145728 | tf_op jit(solution)/shard_map/all_to_all | solution.py:54
  380.7 8.4 %copy-start.12 = (f32[2,512,1536]{2,1,0:T(8,128)}, f32[2,512,1536]{2,1,0:T(8,128)S(1)}, u32[]{:S(2)}) copy-start(f32[2,512,1536]{2,1,0:T(8,128)S(1)} %fusion.4) | copy-start | bytes 18874372
  389.1 6.0 copy-start.37
  389.1 6.0 copy-start.38
  389.1 6.0 copy-start.41
  390.5 23.8 %all-to-all-start.1 = ((bf16[2,2,256,768]{3,2,1,0:T(8,128)(2,1)}), bf16[2,2,256,768]{3,2,1,0:T(8,128)(2,1)}, u32[]{:S(2)}, u32[]{:S(2)}) async-start(bf16[2,2,256,768]{3,2,1,0:T(8,128)(2,1)} %bitcast.212), calls=%async_computation.1 | async-start | bytes 3145728 | tf_op jit(solution)/shard_map/all_to_all | solution.py:54
  416.3 3.6 copy-start.3
  457.1 7.3 %copy-start.39 = (bf16[768]{0:T(1024)(128)(2,1)S(1)}, bf16[768]{0:T(1024)(128)(2,1)}, u32[]{:S(2)}) copy-start(bf16[768]{0:T(1024)(128)(2,1)} %param.45) | copy-start | bytes 4612
  459.8 22.0 %all-to-all-start.3 = ((bf16[2,2,256,768]{3,2,1,0:T(8,128)(2,1)}), bf16[2,2,256,768]{3,2,1,0:T(8,128)(2,1)}, u32[]{:S(2)}, u32[]{:S(2)}) async-start(bf16[2,2,256,768]{3,2,1,0:T(8,128)(2,1)} %bitcast.213), calls=%async_computation.3 | async-start | bytes 3145728 | tf_op jit(solution)/shard_map/all_to_all | solution.py:54
  491.6 6.6 copy-start.14
  511.1 12.4 %copy-start.10 = (bf16[2,256,768]{1,2,0:T(8,128)(2,1)S(1)}, bf16[2,256,768]{1,2,0:T(8,128)(2,1)}, u32[]{:S(2)}) copy-start(bf16[2,256,768]{1,2,0:T(8,128)(2,1)} %copy-done.9) | copy-start | bytes 2359300
  520.8 2.7 copy-start.2
  530.3 5.6 copy-start.7
  530.3 38.9 %all-to-all-start.4 = ((bf16[2,4,256,768]{2,3,1,0:T(8,128)(2,1)}), bf16[2,4,256,768]{2,3,1,0:T(8,128)(2,1)}, u32[]{:S(2)}, u32[]{:S(2)}) async-start(bf16[2,4,256,768]{2,3,1,0:T(8,128)(2,1)} %maximum_bitcast_fusion), calls=%async_computation.4 | async-start | bytes 6291456 | tf_op jit(solution)/shard_map/all_to_all | solution.py:54
  536.0 5.0 copy-start.24
  546.4 25.5 %copy-start.26 = (bf16[8,768]{1,0:T(8,128)(2,1)S(1)}, bf16[8,768]{1,0:T(8,128)(2,1)}, u32[]{:S(2)}) copy-start(bf16[8,768]{1,0:T(8,128)(2,1)} %param.36) | copy-start | bytes 36868
  546.4 25.8 %copy-start.22 = (bf16[2,256,8]{1,2,0:T(8,128)(2,1)S(1)}, bf16[2,256,8]{1,2,0:T(8,128)(2,1)}, u32[]{:S(2)}) copy-start(bf16[2,256,8]{1,2,0:T(8,128)(2,1)} %copy-done.21) | copy-start | bytes 24580
  (8 other events, 13.3 us)
Sparse Core Ops, SparseCore 0:
  13.2 89.1 all-gather.11
  124.0 48.0 all-gather.9
  174.5 50.4 all-gather.7
  228.8 85.8 all-gather.13
where the time goes:
time: 676 us; the launch traced here: 668 us
  waiting for transfers between devices  247 us (37%)
  matrix products  152 us (22%)
  blocking collectives  125 us (18%)
  other arithmetic  59 us (9%)
  local copies, waits for them, and re-layouts  48.2 us (7%)
  starting transfers between devices  22.4 us (3%)
  between operations  15.1 us (2%)
    all_gather x3, waiting for transfers between devices, in_one_piece(): whole = lax.all_gather(both, axis, axis=dim, tiled=True)  146 us
    psum x1, blocking collectives, shards(): lax.psum((local_query, local_value), ('dp', 'tp'))  76.8 us
    all_to_all x4, waiting for transfers between devices, summed_on_arrival(): lax.all_to_all(parts, axis, split_axis=0, concat_axis=0, tiled=True)  56.1 us
    all_gather x1, waiting for transfers between devices, rows_first(): whole, at, outs = (lax.all_gather(both, axis, axis=0, tiled=True), 0, [])  44.9 us
    all_to_all x2, blocking collectives, copy_for_each(): return lax.all_to_all(copies, axis, split_axis=0, concat_axis=0, tiled=True)  43.5 us
    dot_general x2, matrix products, feed_forward(): jnp.dot(hidden_act, down_mat, preferred_element_type=jnp.float32)  27.6 us
    unnamed x99, local copies, waits for them, and re-layouts  26 us
    all_to_all x4, starting transfers between devices, summed_on_arrival(): lax.all_to_all(parts, axis, split_axis=0, concat_axis=0, tiled=True)  18.6 us
  transfers between devices with their start and end apart: 9, of which 7 were waited for; matrix products, arithmetic and copies ran while one was open for 16% of the time, Pallas kernels for 0%

commit v1 on v0

v1 whole, which is shorter than its diff:
```python
import functools
import math

import jax
import jax.numpy as jnp
from jax import lax
from jax.experimental import pallas as pl
from jax.experimental.pallas import tpu as pltpu
from jax.sharding import PartitionSpec as P

HEADS = 12
EPSILON = 1e-05
D = 768
FF = 3072
SEQ = 512
HALF = 256
BLOCK = 48
QKV = 2560
QKV_HALF = QKV // 2
OUT_HALF = D // 2
FEED_HALF = FF
STAGED = QKV_HALF + OUT_HALF + FEED_HALF
HOPS = (1, 3, 2)
MESH = pl.DeviceIdType.MESH
BF16 = jnp.bfloat16
F32 = jnp.float32


def place():
    dp, tp = lax.axis_index("dp"), lax.axis_index("tp")
    core = lax.rem(dp, 2)
    z = lax.rem(lax.div(dp, 2), 4) * 2 + tp
    y = lax.rem(lax.div(dp, 8), 4)
    x = lax.div(dp, 32)
    return x, y, z, core


def device(x, y, z, core):
    return (((x * 4 + y) * 4 + lax.div(z, 2)) * 2 + core, lax.rem(z, 2))


def slot_of(z, core):
    return (lax.div(z, 2) * 2 + core) * 2 + lax.rem(z, 2)


def remote(src, dst, send, recv, target):
    return pltpu.make_async_remote_copy(
        src_ref=src, dst_ref=dst, send_sem=send, recv_sem=recv, device_id=target, device_id_type=MESH
    )


def gather_kernel(
    staged, tokens, eval_tokens, cotangent,
    w_qkv, w_out, w_feed, rows, eval_rows, cots,
    arrived, packed, z_send, z_recv, xy_send, xy_recv, sib_send, sib_recv, pair_send, pair_recv, local_sem,
):
    x, y, z, core = place()
    tp = lax.rem(z, 2)
    sibling = device(x, y, z, 1 - core)
    partner = device(x, y, z + 1 - 2 * tp, core)
    first = core == 0
    u = jnp.where(first, x, y)
    v = jnp.where(first, y, x)

    def at(uu, vv):
        uu, vv = lax.rem(uu, 4), lax.rem(vv, 4)
        return device(jnp.where(first, uu, vv), jnp.where(first, vv, uu), z, core)

    def block(uu, vv):
        uu, vv = lax.rem(uu, 4), lax.rem(vv, 4)
        return jnp.where(first, uu * 4 + vv, vv * 4 + uu)

    column = [(dz, dc) for dz in range(8) for dc in range(2) if (dz, dc) != (0, 0)]
    greet = [device(x, y, lax.rem(z + dz, 8), lax.rem(core + dc, 2)) for dz, dc in column]
    greet += [at(u + h, v) for h in HOPS] + [at(u, v + h) for h in HOPS]
    barrier = pltpu.get_barrier_semaphore()
    for other in greet:
        pl.semaphore_signal(barrier, inc=1, device_id=other, device_id_type=MESH)
    pl.semaphore_wait(barrier, len(greet))

    mine = slot_of(z, core)
    parts = ((0, QKV_HALF), (QKV_HALF, STAGED - QKV_HALF))
    waits = []

    def z_copy(part, n):
        dz, dc = column[n]
        lo, width = parts[part]
        zz, cc = lax.rem(z + dz, 8), lax.rem(core + dc, 2)
        return remote(
            staged.at[cc, :, pl.ds(lo, width)], arrived.at[mine, :, pl.ds(lo, width)],
            z_send.at[part, n], z_recv.at[part, mine], device(x, y, zz, cc),
        )

    def z_arrival(part, n):
        dz, dc = column[n]
        lo, width = parts[part]
        slot = slot_of(lax.rem(z + dz, 8), lax.rem(core + dc, 2))
        return remote(
            staged.at[core, :, pl.ds(lo, width)], arrived.at[slot, :, pl.ds(lo, width)],
            z_send.at[part, n], z_recv.at[part, slot], partner,
        )

    def send(copy):
        copy.start()
        waits.append(copy)

    for n in range(15):
        send(z_copy(0, n))
    pair = []
    t_rows = pl.ds(pl.multiple_of(tp * HALF, HALF), HALF)
    pair.append(remote(tokens.at[1 - tp], rows.at[t_rows], pair_send.at[0], pair_recv.at[0], partner))
    pair.append(remote(eval_tokens, eval_rows.at[:, t_rows], pair_send.at[1], pair_recv.at[1], partner))
    pair.append(remote(cotangent.at[1 - tp], cots.at[t_rows], pair_send.at[2], pair_recv.at[2], partner))
    own = [
        pltpu.make_async_copy(tokens.at[tp], rows.at[t_rows], local_sem.at[0]),
        pltpu.make_async_copy(eval_tokens, eval_rows.at[:, t_rows], local_sem.at[1]),
        pltpu.make_async_copy(cotangent.at[tp], cots.at[t_rows], local_sem.at[2]),
    ]
    for n in range(15):
        send(z_copy(1, n))
    for c in pair + own:
        c.start()
    arrived[pl.ds(mine, 1)] = staged[pl.ds(core, 1)]

    groups = (
        (w_qkv, pl.multiple_of(core * QKV_HALF, 128), QKV_HALF),
        (w_out, pl.multiple_of(core * OUT_HALF, 128), OUT_HALF),
        (w_feed, pl.multiple_of(core * FEED_HALF, 128), FEED_HALF),
    )

    def region(g, uu, vv, other=False):
        ref, lo, width = groups[g]
        if other:
            lo = pl.multiple_of((1 - core) * width, 128)
        return ref.at[pl.ds(pl.multiple_of(block(uu, vv) * BLOCK, BLOCK), BLOCK), pl.ds(lo, width)]

    def pieces(j, k):
        return (u + (4 - HOPS[j - 1] if j else 0), v + (4 - HOPS[k - 1] if k else 0))

    def spread_first(g):
        for k, h in enumerate(HOPS):
            r = region(g, u, v)
            send(remote(r, r, xy_send.at[g, k], xy_recv.at[g, k], at(u + h, v)))

    def spread_second(g, j):
        r = region(g, *pieces(j, 0))
        for k, h in enumerate(HOPS):
            n = 3 + 3 * j + k
            send(remote(r, r, xy_send.at[g, n], xy_recv.at[g, n], at(u, v + h)))

    def to_sibling(g, j, k):
        r = region(g, *pieces(j, k))
        send(remote(r, r, sib_send.at[g, 4 * j + k], sib_recv.at[g, 4 * j + k], sibling))

    def take(g, j, k):
        r = region(g, *pieces(j, k))
        n = 3 + 3 * j + k - 1 if k else j - 1
        remote(r, r, xy_send.at[g, n], xy_recv.at[g, n], partner).wait_recv()

    def take_sibling(g, j, k):
        r = region(g, v + (4 - HOPS[j - 1] if j else 0), u + (4 - HOPS[k - 1] if k else 0), True)
        remote(r, r, sib_send.at[g, 4 * j + k], sib_recv.at[g, 4 * j + k], partner).wait_recv()

    def spread(g):
        spread_first(g)
        spread_second(g, 0)
        to_sibling(g, 0, 0)
        for j in range(1, 4):
            take(g, j, 0)
            spread_second(g, j)
            to_sibling(g, j, 0)

    def finish(g):
        for j in range(4):
            for k in range(1, 4):
                take(g, j, k)
                to_sibling(g, j, k)
        for j in range(4):
            for k in range(4):
                take_sibling(g, j, k)

    here = pl.ds(pl.multiple_of(block(u, v) * BLOCK, BLOCK), BLOCK)
    for n in range(15):
        z_arrival(0, n).wait_recv()
    for s in range(16):
        packed[3 * s : 3 * s + 3, 0:QKV_HALF] = arrived[s, 0:3, 0:QKV_HALF].astype(F32)
    w_qkv[here, pl.ds(pl.multiple_of(core * QKV_HALF, 128), QKV_HALF)] = packed[:, 0:QKV_HALF].astype(BF16)
    spread(0)
    for n in range(15):
        z_arrival(1, n).wait_recv()
    for s in range(16):
        packed[3 * s : 3 * s + 3, 0:OUT_HALF] = arrived[s, 0:3, QKV_HALF : QKV_HALF + OUT_HALF].astype(F32)
    w_out[here, pl.ds(pl.multiple_of(core * OUT_HALF, 128), OUT_HALF)] = packed[:, 0:OUT_HALF].astype(BF16)
    lo = QKV_HALF + OUT_HALF
    for s in range(16):
        part = s % 2
        for half in range(2):
            row = (s // 2) * 6 + half * 3
            for which in range(2):
                src = lo + half * 1536 + which * D
                packed[row : row + 3, which * 1536 + part * D : which * 1536 + part * D + D] = arrived[
                    s, 0:3, src : src + D
                ].astype(F32)
    w_feed[here, pl.ds(pl.multiple_of(core * FEED_HALF, 128), FEED_HALF)] = packed[...].astype(BF16)
    spread(1)
    spread(2)
    finish(0)
    finish(1)
    finish(2)
    for c in pair:
        c.wait()
    for c in own:
        c.wait()
    for c in waits:
        c.wait_send()


def gather_all(staged, tokens, eval_tokens, cotangent):
    out = (
        jax.ShapeDtypeStruct((D, QKV), BF16),
        jax.ShapeDtypeStruct((D, D), BF16),
        jax.ShapeDtypeStruct((D, 2 * FF), BF16),
        jax.ShapeDtypeStruct((SEQ, D), BF16),
        jax.ShapeDtypeStruct((2, SEQ, D), BF16),
        jax.ShapeDtypeStruct((SEQ, D), BF16),
    )
    vmem, hbm = pl.BlockSpec(memory_space=pltpu.VMEM), pl.BlockSpec(memory_space=pl.ANY)
    dma = pltpu.SemaphoreType.DMA
    return pl.pallas_call(
        gather_kernel,
        out_shape=out,
        in_specs=[vmem, hbm, hbm, hbm],
        out_specs=[vmem, vmem, vmem, hbm, hbm, hbm],
        scratch_shapes=[
            pltpu.VMEM((16, 4, STAGED), BF16),
            pltpu.VMEM((BLOCK, FF), F32),
            dma((2, 15)), dma((2, 16)), dma((3, 15)), dma((3, 15)), dma((3, 16)), dma((3, 16)),
            dma((3,)), dma((3,)), dma((3,)),
        ],
        compiler_params=pltpu.CompilerParams(collective_id=0, has_side_effects=True, vmem_limit_bytes=56 << 20),
    )(staged, tokens, eval_tokens, cotangent)


def staged_weights(w_query, w_key, w_value, w_out, w_up, w_down, a_query, a_value):
    def halves(a, count):
        return jnp.moveaxis(a.reshape(3, 2, count), 1, 0)

    blank = functools.partial(jnp.zeros, dtype=BF16)
    qkv = jnp.concatenate([a_query, a_value, blank((3, 112)), w_query, w_key, w_value, blank((3, 128))], axis=1)
    feed = jnp.stack([w_up, w_down.T]).reshape(2, 2, 3, 2, D)
    feed = jnp.transpose(feed, (3, 2, 1, 0, 4)).reshape(2, 3, FF)
    both = jnp.concatenate([halves(qkv, QKV_HALF), halves(w_out, OUT_HALF), feed], axis=2)
    return jnp.pad(both, ((0, 0), (0, 1), (0, 0)))


def norm_rows(rows, gain, shift):
    mean = jnp.mean(rows, axis=-1, keepdims=True)
    centred = rows - mean
    spread = jnp.mean(centred * centred, axis=-1, keepdims=True)
    return centred * lax.rsqrt(spread + EPSILON) * gain + shift


def gelu(u):
    return jax.nn.gelu(u, approximate=False)


def dot(a, b):
    return jnp.dot(a, b, preferred_element_type=F32)


def split_heads(a):
    return a.reshape(*a.shape[:-1], HEADS, D // HEADS)


def attend(query, key, value, valid):
    q, k, v = split_heads(query), split_heads(key), split_heads(value)
    scores = jnp.einsum("nqhe,nkhe->nhqk", q, k, preferred_element_type=F32) * 0.125
    scores = jnp.where(valid[:, None, None, :], scores, -1e30)
    top = jnp.max(scores, axis=-1, keepdims=True)
    e = jnp.exp(scores - top)
    prob = e / jnp.sum(e, axis=-1, keepdims=True)
    mix = jnp.einsum("nhqk,nkhe->nqhe", prob.astype(BF16), v, preferred_element_type=F32)
    return mix.reshape(query.shape).astype(BF16), prob


def shards(
    tokens, eval_tokens, cotangent, lengths, w_query, w_key, w_value, w_out, w_up, w_down, a_query, a_value,
    query_up, value_up, query_bias, value_bias, bias_out, bias_up, bias_down, gain_one, shift_one, gain_two, shift_two,
):
    tp = lax.axis_index("tp")
    staged = staged_weights(w_query, w_key, w_value, w_out, w_up, w_down, a_query, a_value)
    qkv, out_mat, feed, rows, eval_rows, cots = gather_all(staged, tokens, eval_tokens, cotangent)
    up = jnp.concatenate([feed[:, 0:1536], feed[:, FF : FF + 1536]], axis=1)
    down = jnp.concatenate([feed[:, 1536:FF], feed[:, FF + 1536 :]], axis=1)
    b_up = jnp.transpose(bias_up.reshape(2, 2, D), (1, 0, 2)).reshape(FF)
    aq, av = qkv[:, 0:8], qkv[:, 8:16]
    wq, wk, wv = (qkv[:, 128 + n * D : 128 + n * D + D] for n in range(3))
    g1, s1, g2, s2, bo, bu, bd, bq, bv = (
        a.astype(F32) for a in (gain_one, shift_one, gain_two, shift_two, bias_out, b_up, bias_down, query_bias, value_bias)
    )
    merged_q = (wq.astype(F32) + 2.0 * dot(aq, query_up)).astype(BF16)
    merged_v = (wv.astype(F32) + 2.0 * dot(av, value_up)).astype(BF16)
    valid = jnp.arange(SEQ, dtype=jnp.int32)[None, :] < lengths[:, None]

    def after(x, mix):
        first = x.astype(F32) + dot(mix, out_mat) + bo
        normed = norm_rows(first, g1, s1)
        pre = dot(normed.astype(BF16), up) + bu
        second = normed + jnp.einsum("sf,df->sd", gelu(pre).astype(BF16), down, preferred_element_type=F32) + bd
        return first, pre, second, norm_rows(second, g2, s2)

    x = rows
    low_q, low_v = dot(x, aq).astype(BF16), dot(x, av).astype(BF16)
    q = (dot(x, wq) + bq + 2.0 * dot(low_q, query_up)).astype(BF16)
    k = dot(x, wk).astype(BF16)
    v = (dot(x, wv) + bv + 2.0 * dot(low_v, value_up)).astype(BF16)
    my_valid = lax.dynamic_slice_in_dim(valid, tp, 1)
    mix, prob = attend(q[None], k[None], v[None], my_valid)
    first, pre, second, layer = after(x, mix[0])
    cot = cots.astype(F32) * my_valid[0][:, None]
    g_second = jax.vjp(lambda r: norm_rows(r, g2, s2), second)[1](cot)[0]
    g_act = dot(g_second.astype(BF16), down)
    g_pre = jax.vjp(gelu, pre)[1](g_act)[0].astype(BF16)
    g_normed = g_second + jnp.einsum("sf,df->sd", g_pre, up, preferred_element_type=F32)
    g_first = jax.vjp(lambda r: norm_rows(r, g1, s1), first)[1](g_normed)[0]
    g_mix = jnp.einsum("sd,ed->se", g_first.astype(BF16), out_mat, preferred_element_type=F32).astype(BF16)
    gh, vh, kh, qh = split_heads(g_mix), split_heads(v), split_heads(k), split_heads(q)
    prob = prob[0]
    g_prob = jnp.einsum("qhe,khe->hqk", gh, vh, preferred_element_type=F32)
    g_score = (prob * (g_prob - jnp.sum(prob * g_prob, axis=-1, keepdims=True))).astype(BF16)
    gq = (jnp.einsum("hqk,khe->qhe", g_score, kh, preferred_element_type=F32) * 0.125).reshape(SEQ, D).astype(BF16)
    gk = (jnp.einsum("hqk,qhe->khe", g_score, qh, preferred_element_type=F32) * 0.125).reshape(SEQ, D).astype(BF16)
    gv = jnp.einsum("hqk,qhe->khe", prob.astype(BF16), gh, preferred_element_type=F32).reshape(SEQ, D).astype(BF16)

    def back(g, w):
        return jnp.einsum("sd,ed->se", g, w, preferred_element_type=F32)

    igrad = g_first + back(gq, merged_q) + back(gk, wk) + back(gv, merged_v)
    gbq = 2.0 * jnp.einsum("sr,sd->rd", low_q, gq, preferred_element_type=F32)
    gbv = 2.0 * jnp.einsum("sr,sd->rd", low_v, gv, preferred_element_type=F32)
    gbq, gbv = lax.psum((gbq, gbv), ("dp", "tp"))

    layer_low = layer.astype(BF16).reshape(2, HALF, D)
    swap = [(0, 1), (1, 0)]

    def place_rows(a):
        keep = lax.dynamic_index_in_dim(a, tp, 0, keepdims=False)
        got = lax.ppermute(lax.dynamic_index_in_dim(a, 1 - tp, 0, keepdims=False).astype(BF16), "tp", swap)
        got = got.astype(a.dtype)
        return jnp.where(tp == 0, jnp.stack([keep, got]), jnp.stack([got, keep]))

    activations = place_rows(layer_low)
    input_grad = place_rows(igrad.reshape(2, HALF, D))

    eq = dot(eval_tokens, merged_q) + bq
    ek = dot(eval_rows, wk)
    ev = dot(eval_rows, merged_v) + bv
    emix, _ = attend(eq.astype(BF16), ek.astype(BF16), ev.astype(BF16), valid)
    evaluated = after(eval_tokens.reshape(SEQ, D), emix.reshape(SEQ, D))[3].astype(BF16).reshape(2, HALF, D)
    return activations, input_grad, gbq, gbv, evaluated


def solution(mesh):
    rows, frozen, whole = P("dp", "tp", None), P(("dp", "tp"), None), P()
    in_specs = (rows, rows, rows, P("dp"), frozen, frozen, frozen, frozen, P("dp", "tp"), P("tp", "dp"), frozen, frozen)
    in_specs += (whole,) * 11
    out_specs = (rows, rows, whole, whole, rows)
    return jax.shard_map(shards, mesh=mesh, in_specs=in_specs, out_specs=out_specs, check_vma=False)
```

time: 676 us -> 359 us (0.53)
  waiting for transfers between devices: 247 us -> 0.01 us
  Pallas kernels: 0 us -> 79.3 us
  blocking collectives: 125 us -> 76.1 us
  other arithmetic: 59 us -> 17.9 us
  local copies, waits for them, and re-layouts: 48.2 us -> 21.5 us
  starting transfers between devices: 22.4 us -> 1.86 us
  between operations: 15.1 us -> 1.59 us
    all_gather x4 -> x0, waiting for transfers between devices: 191 us -> none  [the longest x3 146 us: in_one_piece(): whole = lax.all_gather(both, axis, axis=dim, tiled=True)]
    pallas_call x0 -> x1, Pallas kernels: none -> 79.3 us  [gather_all(): pl.pallas_call(gather_kernel, out_shape=out, in_specs=[vmem, hbm, hbm, hb...]
    all_to_all x5 -> x0, waiting for transfers between devices: 56.1 us -> none  [the longest x4 56.1 us: summed_on_arrival(): lax.all_to_all(parts, axis, split_axis=0, concat_axis=0, tiled=True)]
    all_to_all x2 -> x0, blocking collectives: 43.5 us -> none  [copy_for_each(): return lax.all_to_all(copies, axis, split_axis=0, concat_axis=0, tiled=True)]
    all_to_all x5 -> x0, starting transfers between devices: 22.2 us -> none  [the longest x4 18.6 us: summed_on_arrival(): lax.all_to_all(parts, axis, split_axis=0, concat_axis=0, tiled=True)]
    unnamed x99 -> x97, local copies, waits for them, and re-layouts: 26 us -> 5.34 us
    another operation x1, other arithmetic: 15.5 us -> 0.05 us  [place_rows(): return jnp.where(tp == 0, jnp.stack([keep, got]), jnp.stack([got, keep]))]
    reduce_sum x10 -> x3, other arithmetic: 20.4 us -> 6.02 us  [the longest x2 5.28 us: norm_rows(): centred = rows - mean]
  transfers between devices with their start and end apart: 9 -> 2, of which waited for: 7 -> 0; matrix products, arithmetic and copies ran while one was open for 16% -> 1% of each run, Pallas kernels for 0% -> 0%
where the time goes in v1:
time: 359 us; the launch traced here: 353 us
  matrix products  155 us (43%)
  Pallas kernels  79.3 us (22%)
  blocking collectives  76.1 us (21%)
  local copies, waits for them, and re-layouts  21.5 us (6%)
  other arithmetic  17.9 us (5%)
    pallas_call x1, Pallas kernels, gather_all(): pl.pallas_call(gather_kernel, out_shape=out, in_specs=[vmem, hbm, hbm, hb...  79.3 us
    psum x1, blocking collectives, shards(): gbq, gbv = lax.psum((gbq, gbv), ('dp', 'tp'))  76.1 us
    dot_general x15, matrix products, dot(): return jnp.dot(a, b, preferred_element_type=F32)  44.5 us
    dot_general x2, matrix products, after(): jnp.einsum('sf,df->sd', gelu(pre).astype(BF16), down, preferred_element_t...  30.3 us
    sub x2, matrix products, attend(): e = jnp.exp(scores - top)  20.4 us
    dot_general x1, matrix products, shards(): jnp.einsum('sf,df->sd', g_pre, up, preferred_element_type=F32)  15.3 us
    dot_general x2, matrix products, attend(): jnp.einsum('nhqk,nkhe->nqhe', prob.astype(BF16), v, preferred_element_typ...  12.1 us
    dot_general x1, matrix products, shards(): g_prob = jnp.einsum('qhe,khe->hqk', gh, vh, preferred_element_type=F32)  9 us
  transfers between devices with their start and end apart: 2, of which 0 were waited for; matrix products, arithmetic and copies ran while one was open for 1% of the time, Pallas kernels for 0%

profile of v1, /device:TPU:1, one launch (start us, length us, event | category | flops | bytes accessed | tf_op | source)
XLA Modules:
  0.0 353.2 jit_solution(14533352400608016745)
XLA Ops:
  3.3 1.4 fusion.91.staged
  4.7 79.3 %shard_map.254 = (bf16[768,2560]{1,0:T(8,128)(2,1)}, bf16[768,768]{1,0:T(8,128)(2,1)}, bf16[768,6144]{1,0:T(8,128)(2,1)}, bf16[512,768]{1,0:T(8,128)(2,1)}, bf16...) custom-call(bf16[2,4,4736]{2,1,0:T(4,128)(2,1)} %fusion.91.staged, bf16[2,256,768]{2,1,0:T(8,128)(2,1)} %tokens.1, ...), custom_call_target="tpu_custom_call" | custom-call | tf_op jit(solution)/shard_map/pallas_call | solution.py:229
  84.0 1.6 convolution_convert_fusion.3
  85.6 3.6 %fusion.58 = f32[512,768]{1,0:T(8,128)} fusion(bf16[512,768]{1,0:T(8,128)(2,1)} %get-tuple-element.11, bf16[768,2560]{1,0:T(8,128)(2,1)} %get-tuple-element.12), kind=kOutput, calls=%fused_computation.117 | convolution fusion | flops 603979776 | bytes 3538944 | tf_op jit(solution)/shard_map/dot_general | solution.py:268
  89.2 1.7 convolution_convert_fusion.2
  91.2 2.0 fusion.60
  93.1 1.4 convolution_convert_fusion
  95.5 3.0 add_convert_fusion.4
  98.6 1.9 add_convert_fusion.3
  100.5 1.0 copy-done.15
  101.5 2.6 add_convert_fusion.1
  104.1 1.7 copy.72
  105.9 3.2 add_convert_fusion.6
  109.1 9.8 %fusion.144 = (f32[2,12,256]{2,1,0:T(8,128)S(1)}, f32[2,12,256,512]{3,2,1,0:T(8,128)}) fusion(pred[2,512]{1,0:T(4,128)(4,1)S(1)} %iota_compare_fusion.1, bf16[2,256,12,64]{1,3,2,0:T(8,128)(2,1)} %bitcast.141, bf16[2,512,12,64]{1,3,2,0:T(8,128)(2,1)S(1)} %bitcast.125), kind=kOutput, calls=%fused_computation.217 | convolution fusion | flops 415236608 | bytes 14967808 | tf_op jit(solution)/shard_map/sub | solution.py:280
  118.9 6.0 %fusion.48 = bf16[2,256,12,64]{1,3,2,0:T(8,128)(2,1)S(1)} fusion(bf16[2,512,12,64]{1,3,2,0:T(8,128)(2,1)S(1)} %bitcast.126, f32[2,12,256,512]{3,2,1,0:T(8,128)} %get-tuple-element.44, f32[2,12,256]{2,1,0:T(8,128)S(1)} %get-tuple-element.43), kind=kOutput, calls=%fused_computation.106 | convolution fusion | flops 409337856 | bytes 14966784 | tf_op jit(solution)/shard_map/nhqk,nkhe->nqhe/dot_general | solution.py:282
  126.8 1.2 copy-done.14
  128.4 3.9 %fusion.140 = (bf16[768,1536]{1,0:T(8,128)(2,1)}, bf16[768,1536]{1,0:T(8,128)(2,1)}, bf16[768,1536]{1,0:T(8,128)(2,1)}, bf16[768,1536]{1,0:T(8,128)(2,1)}) fusion(bf16[768,6144]{1,0:T(8,128)(2,1)S(1)} %bitcast.112), kind=kLoop, calls=%fused_computation.213 | loop fusion | bytes 18874368 | tf_op jit(solution)/shard_map/slice | solution.py:294
  132.5 22.0 %fusion.146 = (f32[512]{0:T(512)S(1)}, f32[512,768]{1,0:T(8,128)S(1)}) fusion(f32[768]{0:T(1024)S(1)} %convert_element_type.223, bf16[768,1536]{1,0:T(8,128)(2,1)} %get-tuple-element.26, bf16[768,1536]{1,0:T(8,128)(2,1)} %get-tuple-element.25, f32[3072]{0:T(1024)S(1)} %reshape.237, bf16[768,1536]{1,0:T(8,128)(2,1)} %get-tuple-element.27, ...), kind=kOutput, calls=%fused_computation.219 | convolution fusion | flops 4959239680 | bytes 12610560 | tf_op jit(solution)/shard_map/sf,df->sd/dot_general | solution.py:309
  154.5 1.9 add_convert_fusion.8
  156.4 1.2 copy.64
  157.9 1.8 add_convert_fusion.9
  159.8 1.2 copy.63
  160.9 10.7 %fusion.141 = (f32[12,512]{1,0:T(8,128)S(1)}, f32[12,512,512]{1,2,0:T(8,128)}) fusion(pred[512]{0:T(512)(128)(4,1)S(1)} %dynamic-slice_reduce_fusion, bf16[512,12,64]{0,2,1:T(8,128)(2,1)} %bitcast.123, bf16[512,12,64]{0,2,1:T(8,128)(2,1)S(1)} %bitcast.113), kind=kOutput, calls=%fused_computation.214 | convolution fusion | flops 415236608 | bytes 14180864 | tf_op jit(solution)/shard_map/sub | solution.py:280
  171.6 6.2 %fusion.37 = bf16[12,64,512]{2,1,0:T(8,128)(2,1)S(1)} fusion(bf16[512,12,64]{0,2,1:T(8,128)(2,1)S(1)} %bitcast.128, f32[12,512,512]{1,2,0:T(8,128)} %get-tuple-element.36, f32[12,512]{1,0:T(8,128)S(1)} %get-tuple-element.35), kind=kOutput, calls=%fused_computation.100 | convolution fusion | flops 409337856 | bytes 14180352 | tf_op jit(solution)/shard_map/nhqk,nkhe->nqhe/dot_general | solution.py:282
  177.8 0.9 fusion.142
  179.4 1.3 copy-done.13
  180.7 17.7 %fusion.4 = (f32[512,3072]{1,0:T(8,128)S(1)}, f32[512,3072]{1,0:T(8,128)}) fusion(f32[3072]{0:T(1024)S(1)} %reshape.237, bf16[768,1536]{1,0:T(8,128)(2,1)S(1)} %copy-done.12, bf16[768,1536]{1,0:T(8,128)(2,1)S(1)} %copy-done.13, f32[512,768]{1,0:T(8,128)S(1)} %get-tuple-element.38, f32[768]{0:T(1024)S(1)} %convert_element_type.216, ...), kind=kOutput, calls=%fused_computation.13 | convolution fusion | flops 2526412800 | bytes 18896896 | tf_op jit(solution)/shard_map/dot_general | solution.py:268
  198.4 8.2 %fusion.143 = (f32[512]{0:T(512)S(1)}, f32[512,768]{1,0:T(8,128)S(1)}) fusion(f32[768]{0:T(1024)S(1)} %convert_element_type.223, bf16[768,1536]{1,0:T(8,128)(2,1)S(1)} %copy-done.11, bf16[768,1536]{1,0:T(8,128)(2,1)S(1)} %copy-done.10, f32[512,3072]{1,0:T(8,128)S(1)} %get-tuple-element.39, f32[512,3072]{1,0:T(8,128)} %get-tuple-element.40, ...), kind=kOutput, calls=%fused_computation.216 | convolution fusion | flops 2434399744 | bytes 20474880 | tf_op jit(solution)/shard_map/sf,df->sd/dot_general | solution.py:309
  207.8 2.8 fusion.139
  210.6 15.3 %multiply_reduce_fusion.3 = (f32[512]{0:T(512)S(1)}, f32[512,768]{1,0:T(8,128)}) fusion(f32[512,768]{1,0:T(8,128)} %copy-done.2, f32[512]{0:T(512)S(1)} %broadcast_multiply_fusion.3, f32[768]{0:T(1024)S(1)} %convert_element_type.215, bf16[768,1536]{1,0:T(8,128)(2,1)} %get-tuple-element.27, bf16[768,1536]{1,0:T(8,128)(2,1)} %get-tuple-element.28, ...), kind=kOutput, calls=%fused_computation.84 | convolution fusion | flops 4877450752 | bytes 26760192 | tf_op jit(solution)/shard_map/sf,df->sd/dot_general | solution.py:324
  225.9 2.5 fusion.138
  228.4 1.7 convolution_convert_fusion.1
  230.2 2.4 copy.68
  232.6 7.9 %fusion.40 = bf16[12,64,512]{2,1,0:T(8,128)(2,1)} fusion(bf16[512,12,64]{0,2,1:T(8,128)(2,1)} %bitcast.130, f32[12,512,512]{1,2,0:T(8,128)} %get-tuple-element.36, f32[12,512]{1,0:T(8,128)S(1)} %get-tuple-element.35), kind=kOutput, calls=%fused_computation.101 | convolution fusion | flops 409337856 | bytes 14180352 | tf_op jit(solution)/shard_map/hqk,qhe->khe/dot_general | solution.py:333
  240.5 9.0 %multiply_reduce_fusion = (f32[12,512]{1,0:T(8,128)S(1)}, f32[12,512,512]{1,2,0:T(8,128)}) fusion(f32[12,512,512]{1,2,0:T(8,128)} %get-tuple-element.36, f32[12,512]{1,0:T(8,128)S(1)} %get-tuple-element.35, bf16[512,12,64]{0,2,1:T(8,128)(2,1)S(1)} %bitcast.131, bf16[512,12,64]{0,2,1:T(8,128)(2,1)S(1)} %bitcast.129), kind=kOutput, calls=%fused_computation.6 | convolution fusion | flops 412084224 | bytes 26787840 | tf_op jit(solution)/shard_map/qhe,khe->hqk/dot_general | solution.py:329
  249.5 7.0 %multiply_convert_fusion = bf16[12,512,512]{1,2,0:T(8,128)(2,1)S(1)} fusion(f32[12,512,512]{1,2,0:T(8,128)} %get-tuple-element.52, f32[12,512]{1,0:T(8,128)S(1)} %get-tuple-element.51, f32[12,512,512]{1,2,0:T(8,128)S(1)} %bitcast.110, f32[12,512]{1,0:T(8,128)S(1)} %get-tuple-element.35), kind=kLoop, calls=%fused_computation.5 | loop fusion | flops 12582912 | bytes 31506432 | tf_op jit(solution)/shard_map/convert_element_type | solution.py:330
  256.5 1.1 multiply_convert_fusion.4
  257.7 2.0 multiply_convert_fusion.3
  259.7 2.0 fusion.149
  261.7 3.2 fusion.63
  265.0 3.4 add_add_fusion.3
  268.4 1.1 copy-done.3
  269.6 1.7 collective-permute-start.1
  272.4 1.0 convolution_multiply_fusion.1
  273.4 76.1 %all-reduce.1 = (f32[8,768]{1,0:T(8,128)}, f32[8,768]{1,0:T(8,128)}) all-reduce(f32[8,768]{1,0:T(8,128)S(1)} %convolution_multiply_fusion.1, f32[8,768]{1,0:T(8,128)} %convolution_multiply_fusion), channel_id=1, replica_groups=mesh['dp'=128,'tp'=2] {'dp','tp'}, use_global_device_ids=true, to_apply=%region_11.12 | all-reduce | flops 12288 | bytes 98304 | tf_op jit(solution)/shard_map/psum | solution.py:341
  349.5 1.2 constant_dynamic-slice_fusion
  350.8 1.2 maximum_select_fusion
  352.0 1.0 maximum_select_fusion.1
  (145 shorter events, 9.7 us)
Async XLA Ops:
  0.6 94.8 %copy-start = (bf16[8,768]{1,0:T(8,128)(2,1)S(1)}, bf16[8,768]{1,0:T(8,128)(2,1)}, u32[]{:S(2)}) copy-start(bf16[8,768]{1,0:T(8,128)(2,1)} %param.35) | copy-start | bytes 36868
  84.0 5.2 %copy-start.7 = (bf16[512,768]{1,0:T(8,128)(2,1)S(1)}, bf16[512,768]{1,0:T(8,128)(2,1)}, u32[]{:S(2)}) copy-start(bf16[512,768]{1,0:T(8,128)(2,1)} %get-tuple-element.11) | copy-start | bytes 2359300
  84.0 5.2 %copy-start.23 = (bf16[768,2560]{1,0:T(8,128)(2,1)S(1)}, bf16[768,2560]{1,0:T(8,128)(2,1)}, u32[]{:S(2)}) copy-start(bf16[768,2560]{1,0:T(8,128)(2,1)} %get-tuple-element.12) | copy-start | bytes 11796484
  85.6 69.0 %copy-start.20 = (bf16[512,8]{0,1:T(8,128)(2,1)}, bf16[512,8]{0,1:T(8,128)(2,1)S(1)}, u32[]{:S(2)}) copy-start(bf16[512,8]{0,1:T(8,128)(2,1)S(1)} %convolution_convert_fusion.3) | copy-start | bytes 24580
  89.2 4.0 %copy-start.35 = (bf16[2,512,768]{2,1,0:T(8,128)(2,1)S(1)}, bf16[2,512,768]{2,1,0:T(8,128)(2,1)}, u32[]{:S(2)}) copy-start(bf16[2,512,768]{2,1,0:T(8,128)(2,1)} %get-tuple-element.16) | copy-start | bytes 4718596
  91.2 66.7 %copy-start.21 = (bf16[512,8]{0,1:T(8,128)(2,1)}, bf16[512,8]{0,1:T(8,128)(2,1)S(1)}, u32[]{:S(2)}) copy-start(bf16[512,8]{0,1:T(8,128)(2,1)S(1)} %convolution_convert_fusion.4) | copy-start | bytes 24580
  94.5 4.0 %copy-start.26 = (bf16[768]{0:T(1024)(128)(2,1)S(1)}, bf16[768]{0:T(1024)(128)(2,1)}, u32[]{:S(2)}) copy-start(bf16[768]{0:T(1024)(128)(2,1)} %param.37) | copy-start | bytes 4612
  94.6 4.0 %copy-start.34 = (s32[2]{0:T(128)S(1)}, s32[2]{0:T(128)}, u32[]{:S(2)}) copy-start(s32[2]{0:T(128)} %param.26) | copy-start | bytes 28
  94.6 4.0 %copy-start.24 = (bf16[8,768]{1,0:T(8,128)(2,1)S(1)}, bf16[8,768]{1,0:T(8,128)(2,1)}, u32[]{:S(2)}) copy-start(bf16[8,768]{1,0:T(8,128)(2,1)} %param.36) | copy-start | bytes 36868
  94.6 5.9 %copy-start.27 = (bf16[768]{0:T(1024)(128)(2,1)S(1)}, bf16[768]{0:T(1024)(128)(2,1)}, u32[]{:S(2)}) copy-start(bf16[768]{0:T(1024)(128)(2,1)} %param.38) | copy-start | bytes 4612
  95.5 6.1 %copy-start.36 = (bf16[2,512,768]{2,1,0:T(8,128)(2,1)S(1)}, bf16[2,512,768]{2,1,0:T(8,128)(2,1)}, u32[]{:S(2)}) copy-start(bf16[2,512,768]{2,1,0:T(8,128)(2,1)} %get-tuple-element.16) | copy-start | bytes 4718596
  118.8 9.5 %slice-start.3 = ((s8[9437184]{0:T(1024)(128)(4,1)}), s8[4194304]{0:T(1024)(128)(4,1)S(1)}, s32[]{:S(2)}) async-start(s8[9437184]{0:T(1024)(128)(4,1)} %bitcast.111), calls=%async_computation.3 | async-start | bytes 8388608
  118.8 7.0 %copy-start.28 = (bf16[768]{0:T(1024)(128)(2,1)S(1)}, bf16[768]{0:T(1024)(128)(2,1)}, u32[]{:S(2)}) copy-start(bf16[768]{0:T(1024)(128)(2,1)} %param.39) | copy-start | bytes 4612
  118.8 7.0 %copy-start.19 = (bf16[2,256,768]{2,1,0:T(8,128)(2,1)S(1)}, bf16[2,256,768]{2,1,0:T(8,128)(2,1)}, u32[]{:S(2)}) copy-start(bf16[2,256,768]{2,1,0:T(8,128)(2,1)} %eval_tokens.1) | copy-start | bytes 2359300
  118.8 7.0 %copy-start.37 = (bf16[768,768]{1,0:T(8,128)(2,1)S(1)}, bf16[768,768]{1,0:T(8,128)(2,1)}, u32[]{:S(2)}) copy-start(bf16[768,768]{1,0:T(8,128)(2,1)} %get-tuple-element.13) | copy-start | bytes 3538948
  118.8 9.5 %slice-start.4 = ((s8[9437184]{0:T(1024)(128)(4,1)}), s8[4194304]{0:T(1024)(128)(4,1)S(1)}, s32[]{:S(2)}) async-start(s8[9437184]{0:T(1024)(128)(4,1)} %bitcast.111), calls=%async_computation.4 | async-start | bytes 8388608
  118.9 9.5 %slice-start.5 = ((s8[9437184]{0:T(1024)(128)(4,1)}), s8[1048576]{0:T(1024)(128)(4,1)S(1)}, s32[]{:S(2)}) async-start(s8[9437184]{0:T(1024)(128)(4,1)} %bitcast.111), calls=%async_computation.5 | async-start | bytes 2097152
  126.8 1.2 copy-start.14
  128.4 4.0 %copy-start.25 = (bf16[3072]{0:T(1024)(128)(2,1)S(1)}, bf16[3072]{0:T(1024)(128)(2,1)}, u32[]{:S(2)}) copy-start(bf16[3072]{0:T(1024)(128)(2,1)} %param.40) | copy-start | bytes 18436
  128.4 4.0 %copy-start.29 = (bf16[768]{0:T(1024)(128)(2,1)S(1)}, bf16[768]{0:T(1024)(128)(2,1)}, u32[]{:S(2)}) copy-start(bf16[768]{0:T(1024)(128)(2,1)} %param.42) | copy-start | bytes 4612
  128.4 4.1 %copy-start.30 = (bf16[768]{0:T(1024)(128)(2,1)S(1)}, bf16[768]{0:T(1024)(128)(2,1)}, u32[]{:S(2)}) copy-start(bf16[768]{0:T(1024)(128)(2,1)} %param.43) | copy-start | bytes 4612
  128.4 4.1 %copy-start.31 = (bf16[768]{0:T(1024)(128)(2,1)S(1)}, bf16[768]{0:T(1024)(128)(2,1)}, u32[]{:S(2)}) copy-start(bf16[768]{0:T(1024)(128)(2,1)} %param.41) | copy-start | bytes 4612
  154.5 3.1 copy-start.17
  160.9 10.7 %copy-start.16 = (bf16[512,768]{0,1:T(8,128)(2,1)S(1)}, bf16[512,768]{0,1:T(8,128)(2,1)}, u32[]{:S(2)}) copy-start(bf16[512,768]{0,1:T(8,128)(2,1)} %copy.63) | copy-start | bytes 2359300
  171.6 6.2 %copy-start.8 = (bf16[512,768]{1,0:T(8,128)(2,1)S(1)}, bf16[512,768]{1,0:T(8,128)(2,1)}, u32[]{:S(2)}) copy-start(bf16[512,768]{1,0:T(8,128)(2,1)} %get-tuple-element.11) | copy-start | bytes 2359300
  171.6 6.2 %copy-start.38 = (bf16[768,768]{1,0:T(8,128)(2,1)S(1)}, bf16[768,768]{1,0:T(8,128)(2,1)}, u32[]{:S(2)}) copy-start(bf16[768,768]{1,0:T(8,128)(2,1)} %get-tuple-element.13) | copy-start | bytes 3538948
  177.8 1.7 copy-start.12
  177.8 2.9 copy-start.13
  178.7 19.6 %copy-start.2 = (f32[512,768]{1,0:T(8,128)}, f32[512,768]{1,0:T(8,128)S(1)}, u32[]{:S(2)}) copy-start(f32[512,768]{1,0:T(8,128)S(1)} %get-tuple-element.38) | copy-start | bytes 4718596
  180.7 17.7 %copy-start.10 = (bf16[768,1536]{1,0:T(8,128)(2,1)S(1)}, bf16[768,1536]{1,0:T(8,128)(2,1)}, u32[]{:S(2)}) copy-start(bf16[768,1536]{1,0:T(8,128)(2,1)} %get-tuple-element.25) | copy-start | bytes 7077892
  180.7 17.7 %copy-start.11 = (bf16[768,1536]{1,0:T(8,128)(2,1)S(1)}, bf16[768,1536]{1,0:T(8,128)(2,1)}, u32[]{:S(2)}) copy-start(bf16[768,1536]{1,0:T(8,128)(2,1)} %get-tuple-element.26) | copy-start | bytes 7077892
  198.4 8.3 %copy-start.41 = (f32[512,3072]{1,0:T(8,128)}, f32[512,3072]{1,0:T(8,128)S(1)}, u32[]{:S(2)}) copy-start(f32[512,3072]{1,0:T(8,128)S(1)} %get-tuple-element.39) | copy-start | bytes 18874372
  198.4 8.3 %copy-start.32 = (bf16[768]{0:T(1024)(128)(2,1)S(1)}, bf16[768]{0:T(1024)(128)(2,1)}, u32[]{:S(2)}) copy-start(bf16[768]{0:T(1024)(128)(2,1)} %param.44) | copy-start | bytes 4612
  198.4 8.3 %copy-start.33 = (bf16[768]{0:T(1024)(128)(2,1)S(1)}, bf16[768]{0:T(1024)(128)(2,1)}, u32[]{:S(2)}) copy-start(bf16[768]{0:T(1024)(128)(2,1)} %param.45) | copy-start | bytes 4612
  198.4 8.6 %copy-start.5 = (bf16[512,768]{1,0:T(8,128)(2,1)S(1)}, bf16[512,768]{1,0:T(8,128)(2,1)}, u32[]{:S(2)}) copy-start(bf16[512,768]{1,0:T(8,128)(2,1)} %get-tuple-element.15) | copy-start | bytes 2359300
  225.9 2.5 copy-start.39
  232.5 7.9 %copy-start.18 = (bf16[512,768]{0,1:T(8,128)(2,1)S(1)}, bf16[512,768]{0,1:T(8,128)(2,1)}, u32[]{:S(2)}) copy-start(bf16[512,768]{0,1:T(8,128)(2,1)} %copy.68) | copy-start | bytes 2359300
  232.5 16.9 %slice-start = ((s8[12582912]{0:T(1024)(128)(4,1)}), s8[4194304]{0:T(1024)(128)(4,1)S(1)}, s32[]{:S(2)}) async-start(s8[12582912]{0:T(1024)(128)(4,1)} %bitcast.109), calls=%async_computation | async-start | bytes 8388608
  232.6 17.0 %slice-start.1 = ((s8[12582912]{0:T(1024)(128)(4,1)}), s8[4194304]{0:T(1024)(128)(4,1)S(1)}, s32[]{:S(2)}) async-start(s8[12582912]{0:T(1024)(128)(4,1)} %bitcast.109), calls=%async_computation.1 | async-start | bytes 8388608
  240.5 9.0 %slice-start.2 = ((s8[12582912]{0:T(1024)(128)(4,1)}), s8[4194304]{0:T(1024)(128)(4,1)S(1)}, s32[]{:S(2)}) async-start(s8[12582912]{0:T(1024)(128)(4,1)} %bitcast.109), calls=%async_computation.2 | async-start | bytes 8388608
  256.5 1.1 copy-start.9
  257.7 2.0 copy-start.40
  259.7 5.3 %copy-start.4 = (bf16[12,64,512]{2,1,0:T(8,128)(2,1)S(1)}, bf16[12,64,512]{2,1,0:T(8,128)(2,1)}, u32[]{:S(2)}) copy-start(bf16[12,64,512]{2,1,0:T(8,128)(2,1)} %fusion.40) | copy-start | bytes 2359300
  265.0 6.3 %copy-start.6 = (bf16[512,768]{1,0:T(8,128)(2,1)S(1)}, bf16[512,768]{1,0:T(8,128)(2,1)}, u32[]{:S(2)}) copy-start(bf16[512,768]{1,0:T(8,128)(2,1)} %get-tuple-element.29) | copy-start | bytes 2359300
  265.0 6.5 %copy-start.22 = (bf16[512,8]{0,1:T(8,128)(2,1)S(1)}, bf16[512,8]{0,1:T(8,128)(2,1)}, u32[]{:S(2)}) copy-start(bf16[512,8]{0,1:T(8,128)(2,1)} %copy-done.21) | copy-start | bytes 24580
  269.6 81.1 %collective-permute-start.1 = (bf16[256,768]{1,0:T(8,128)(2,1)S(1)}, bf16[256,768]{1,0:T(8,128)(2,1)S(1)}, u32[]{:S(2)}, u32[]{:S(2)}) collective-permute-start(bf16[256,768]{1,0:T(8,128)(2,1)S(1)} %fusion.82), channel_id=1, source_target_pairs={{0,1},{1,0},{2,3},{3,2},{4,5},{5,4},{6,7},{7,6},{8,9},{9,8},{10,11... | collective-permute-start | bytes 1179656 | tf_op jit(solution)/shard_map/ppermute | solution.py:348
  271.4 80.7 %collective-permute-start = (bf16[256,768]{1,0:T(8,128)(2,1)S(1)}, bf16[256,768]{1,0:T(8,128)(2,1)S(1)}, u32[]{:S(2)}, u32[]{:S(2)}) collective-permute-start(bf16[256,768]{1,0:T(8,128)(2,1)S(1)} %get-tuple-element.31), channel_id=1, source_target_pairs={{0,1},{1,0},{2,3},{3,2},{4,5},{5,4},{6,7},{7,6},{8,9},{9,8},{10,11... | collective-permute-start | bytes 1179656 | tf_op jit(solution)/shard_map/ppermute | solution.py:348
  272.4 80.6 %copy-start.1 = (bf16[8,768]{1,0:T(8,128)(2,1)S(1)}, bf16[8,768]{1,0:T(8,128)(2,1)}, u32[]{:S(2)}) copy-start(bf16[8,768]{1,0:T(8,128)(2,1)} %param.35) | copy-start | bytes 36868
  (2 other events, 2.2 us)
